TPU v7x, 512 devices: a whole 4x8x8 slice. The times are simulated.
512 devices in a mesh: tm: 128 (over y, x_hi, z), head: 4 (over x_lo, core).
Axes of the slice: x: 4 (x_hi: 2, x_lo: 2; x = x_hi * 2 + x_lo), y: 8, z: 8, core: 2. Of those that a mesh axis runs over, the one named last changes fastest.
Arguments:
- hidden_states: bfloat16 [16384, 1280], P('tm', 'head'), may hold values from -24 to 24
- w_query: bfloat16 [1280, 1280], P(None, 'head'), may hold values from -1 to 1, as said below
- w_key: bfloat16 [1280, 1280], P(None, 'head'), may hold values from -1 to 1, as said below
- w_value: bfloat16 [1280, 1280], P(None, 'head'), may hold values from -0.15625 to 0.15625
- grad_out: bfloat16 [16384, 1280], P('tm', 'head'), may hold values from -6 to 6
Outputs:
- attended: bfloat16 [16384, 1280], P('tm', 'head')
- grad_query_weight: bfloat16 [1280, 1280], P(None, 'head')
- grad_hidden: bfloat16 [16384, 1280], P('tm', 'head')
Inputs may be any that keep to these rules, and one draw needn't show every extreme that they name: `w_query`: entries of order 1280 ** -0.5. `w_key`: entries of order 1280 ** -0.5.
All inputs are finite; a program needn't handle non-finite values.
Results may differ from a plain program's by a relative error of at most 0.018.
Values may be sent and summed in bfloat16 or wider, within the bound.
A program may use at most 128 MiB of HBM per device.

v0:
```python
import jax
import jax.numpy as jnp
from jax import lax
from jax.sharding import PartitionSpec as P

P_SIZE = 64
CLIP = 8
HD = 64


def shifted(value, axis, steps):
    count = lax.axis_size(axis)
    initial, last = (max(0, -steps), min(count, count - steps))
    return lax.ppermute(value, axis, [(source, source + steps) for source in range(initial, last)])


def carried_in(shard, axis, join, neutral):
    count = lax.axis_size(axis)
    place = lax.axis_index(axis)
    ahead = count - 1 - place
    gathered = jax.tree.map(
        lambda a, kind: lax.all_gather(a.astype(kind), axis),
        shard,
        (jnp.bfloat16, jnp.bfloat16, jnp.bfloat16),
    )
    state = jax.tree.map(lambda a, e: jnp.zeros_like(a) + jnp.asarray(e, a.dtype), shard, neutral)

    def one(step, state):
        source = count - 1 - step
        return join(
            state,
            jax.tree.map(
                lambda a, own: lax.dynamic_index_in_dim(a, source, 0, False).astype(own.dtype),
                gathered,
                shard,
            ),
        )

    return lax.fori_loop(0, ahead, one, state)


def project(rows, weight):
    return jnp.dot(rows, weight, preferred_element_type=jnp.float32).astype(jnp.bfloat16)


def segment_add(earlier, later):
    flag = jnp.maximum(earlier[0], later[0])
    keep = 1.0 - later[0]
    return (flag, later[1] + keep * earlier[1], later[2] + keep * earlier[2])


def shards(hidden_states, w_query, w_key, w_value, grad_out):
    scale = HD ** (-0.5)
    width = w_query.shape[1]
    heads_here = width // HD
    frames_here = hidden_states.shape[0] // P_SIZE
    span = CLIP // frames_here
    levels = span.bit_length() - 1
    shape_four = (frames_here, P_SIZE, heads_here, HD)
    shape_three = (P_SIZE, heads_here, HD)
    position = lax.axis_index("tm") % span
    first = position == 0
    last = position == span - 1
    features = lax.all_gather(hidden_states, "head", axis=1, tiled=True)
    query = project(features, w_query)
    key = project(features, w_key)
    value = project(features, w_value)
    anchor_key, anchor_value = (key[:P_SIZE], value[:P_SIZE])
    for level in range(levels):
        reach = 1 << level
        got_key, got_value = shifted((anchor_key, anchor_value), "tm", reach)
        take = (position >= reach) & (position < 2 * reach)
        anchor_key = jnp.where(take, got_key, anchor_key)
        anchor_value = jnp.where(take, got_value, anchor_value)
    left_key, left_value = shifted((key[-P_SIZE:], value[-P_SIZE:]), "tm", 1)
    edge_key = jnp.where(first, anchor_key, left_key)
    edge_value = jnp.where(first, anchor_value, left_value)
    prior_key = jnp.concatenate([edge_key, key[:-P_SIZE]], 0).reshape(shape_four)
    prior_value = jnp.concatenate([edge_value, value[:-P_SIZE]], 0).reshape(shape_four)
    lead_key = anchor_key.reshape(shape_three)
    lead_value = anchor_value.reshape(shape_three)
    queries = query.reshape(shape_four)
    cotan = grad_out.reshape(shape_four)
    score_lead = (
        jnp.einsum("fqhd,khd->fhqk", queries, lead_key, preferred_element_type=jnp.float32) * scale
    )
    score_prior = (
        jnp.einsum("fqhd,fkhd->fhqk", queries, prior_key, preferred_element_type=jnp.float32)
        * scale
    )
    top = jnp.maximum(
        jnp.max(score_lead, -1, keepdims=True), jnp.max(score_prior, -1, keepdims=True)
    )
    exp_lead = jnp.exp(score_lead - top)
    exp_prior = jnp.exp(score_prior - top)
    denom = jnp.sum(exp_lead, -1, keepdims=True) + jnp.sum(exp_prior, -1, keepdims=True)
    prob_lead = exp_lead / denom
    prob_prior = exp_prior / denom
    lead_b = prob_lead.astype(jnp.bfloat16)
    prior_b = prob_prior.astype(jnp.bfloat16)
    attended = jnp.einsum("fhqk,khd->fqhd", lead_b, lead_value, preferred_element_type=jnp.float32)
    attended = attended + jnp.einsum(
        "fhqk,fkhd->fqhd", prior_b, prior_value, preferred_element_type=jnp.float32
    )
    attended = attended.astype(jnp.bfloat16).reshape(frames_here * P_SIZE, width)
    dprob_lead = jnp.einsum("fqhd,khd->fhqk", cotan, lead_value, preferred_element_type=jnp.float32)
    dprob_prior = jnp.einsum(
        "fqhd,fkhd->fhqk", cotan, prior_value, preferred_element_type=jnp.float32
    )
    inner = jnp.sum(prob_lead * dprob_lead, -1, keepdims=True) + jnp.sum(
        prob_prior * dprob_prior, -1, keepdims=True
    )
    dlead_b = (prob_lead * (dprob_lead - inner) * scale).astype(jnp.bfloat16)
    dprior_b = (prob_prior * (dprob_prior - inner) * scale).astype(jnp.bfloat16)
    dquery = jnp.einsum("fhqk,khd->fqhd", dlead_b, lead_key, preferred_element_type=jnp.float32)
    dquery = dquery + jnp.einsum(
        "fhqk,fkhd->fqhd", dprior_b, prior_key, preferred_element_type=jnp.float32
    )
    dquery = dquery.astype(jnp.bfloat16).reshape(frames_here * P_SIZE, width)
    lead_dkey = jnp.einsum(
        "fhqk,fqhd->khd", dlead_b, queries, preferred_element_type=jnp.float32
    ).reshape(P_SIZE, width)
    lead_dvalue = jnp.einsum(
        "fhqk,fqhd->khd", lead_b, cotan, preferred_element_type=jnp.float32
    ).reshape(P_SIZE, width)
    before_dkey = jnp.einsum(
        "fhqk,fqhd->fkhd", dprior_b, queries, preferred_element_type=jnp.float32
    ).reshape(frames_here, P_SIZE, width)
    before_dvalue = jnp.einsum(
        "fhqk,fqhd->fkhd", prior_b, cotan, preferred_element_type=jnp.float32
    ).reshape(frames_here, P_SIZE, width)
    weight_part = jnp.einsum("rc,rw->cw", features, dquery, preferred_element_type=jnp.float32)
    grad_weight = lax.psum(weight_part, "tm")
    zeros_frame = jnp.zeros_like(lead_dkey)
    start_flag = jnp.where(first, 1.0, 0.0).astype(jnp.float32)
    sent_dkey = jnp.where(first, zeros_frame, lead_dkey)
    sent_dvalue = jnp.where(first, zeros_frame, lead_dvalue)
    _, later_dkey, later_dvalue = carried_in(
        (start_flag, sent_dkey, sent_dvalue),
        "tm",
        segment_add,
        (jnp.zeros((), jnp.float32), zeros_frame, zeros_frame),
    )
    right_dkey, right_dvalue = (
        shifted(before_dkey[0].astype(jnp.bfloat16), "tm", -1).astype(jnp.float32),
        shifted(before_dvalue[0].astype(jnp.bfloat16), "tm", -1).astype(jnp.float32),
    )
    right_dkey = jnp.where(last, zeros_frame, right_dkey)
    right_dvalue = jnp.where(last, zeros_frame, right_dvalue)
    total_dkey = jnp.concatenate([before_dkey[1:], right_dkey[None]], 0)
    total_dvalue = jnp.concatenate([before_dvalue[1:], right_dvalue[None]], 0)
    total_dkey = total_dkey.at[0].add(
        jnp.where(first, lead_dkey + later_dkey + before_dkey[0], zeros_frame)
    )
    total_dvalue = total_dvalue.at[0].add(
        jnp.where(first, lead_dvalue + later_dvalue + before_dvalue[0], zeros_frame)
    )
    dkey = total_dkey.astype(jnp.bfloat16).reshape(frames_here * P_SIZE, width)
    dvalue = total_dvalue.astype(jnp.bfloat16).reshape(frames_here * P_SIZE, width)
    partial_value = jnp.einsum("rw,cw->rc", dquery, w_query, preferred_element_type=jnp.float32)
    partial_value = partial_value + jnp.einsum(
        "rw,cw->rc", dkey, w_key, preferred_element_type=jnp.float32
    )
    partial_value = partial_value + jnp.einsum(
        "rw,cw->rc", dvalue, w_value, preferred_element_type=jnp.float32
    )
    grad_hidden = lax.psum_scatter(
        partial_value.astype(jnp.bfloat16), "head", scatter_dimension=1, tiled=True
    )
    return (attended, grad_weight.astype(jnp.bfloat16), grad_hidden)


def solution(mesh):
    placed = (P("tm", "head"), P(None, "head"), P(None, "head"), P(None, "head"), P("tm", "head"))
    return jax.shard_map(
        shards,
        mesh=mesh,
        in_specs=placed,
        out_specs=(P("tm", "head"), P(None, "head"), P("tm", "head")),
        check_vma=False,
    )
```

profile of v0, /device:TPU:2, one launch (start us, length us, event | category | flops | bytes accessed | tf_op | source)
XLA Modules:
  0.0 1526.2 jit_solution(7963021348517703956)
XLA Ops:
  7.2 10.9 all_gather.17
  18.1 1.6 convolution_convert_fusion
  19.7 1.3 collective-permute-start.2
  21.0 1.7 collective-permute-done.2
  22.8 4.4 collective-permute-start.4
  27.2 5.6 collective-permute-start.3
  38.0 5.5 collective-permute-start
  43.4 1.7 collective-permute-done
  45.2 4.2 collective-permute-start.5
  49.4 5.1 collective-permute-start.1
  54.6 1.7 collective-permute-done.1
  59.3 1.3 dynamic-slice.16
  61.3 359.7 %all-reduce = bf16[128]{0:T(256)(128)(2,1)} all-reduce(bf16[128]{0:T(256)(128)(2,1)S(1)} %dynamic-update-slice.6), channel_id=1, replica_groups=mesh['tm'=128,'head'=4] {'tm'}, use_global_device_ids=true, to_apply=%add | all-reduce | flops 128 | bytes 512
  422.8 1.3 collective-permute-start.7
  424.9 1.4 fusion.32
  427.3 1.7 copy.203
  431.5 1.7 copy.193
  435.0 1.3 collective-permute-start.6
  437.8 1.5 pad_maximum_fusion.1
  439.3 2.5 collective-permute-done.6
  441.9 351.5 %while.18 = (s32[]{:T(128)}, f32[64,320]{1,0:T(8,128)S(1)}, f32[64,320]{1,0:T(8,128)S(1)}, s32[]{:T(128)}, bf16[128,64,320]{2,1,0:T(8,128)(2,1)}, /*index=5*/bf1...) while((s32[]{:T(128)}, f32[64,320]{1,0:T(8,128)S(1)}, ...), condition=%wide.region_8.9_spmd, body=%wide.region_7.8_spmd.sunk | while | flops 122887 | bytes 409797 | solution.py:39
  441.9 1.2 dynamic_slice.28
  444.7 1.2 dynamic_slice.28
  447.5 1.2 dynamic_slice.28
  450.2 1.2 dynamic_slice.28
  458.5 1.2 dynamic_slice.28
  477.9 1.2 dynamic_slice.28
  497.3 1.2 dynamic_slice.28
  511.1 1.2 dynamic_slice.28
  530.5 1.2 dynamic_slice.28
  549.9 1.2 dynamic_slice.28
  563.7 1.2 dynamic_slice.28
  583.1 1.2 dynamic_slice.28
  602.4 1.2 dynamic_slice.28
  616.3 1.2 dynamic_slice.28
  635.6 1.2 dynamic_slice.28
  655.0 1.2 dynamic_slice.28
  668.9 1.2 dynamic_slice.28
  688.2 1.2 dynamic_slice.28
  707.6 1.2 dynamic_slice.28
  721.4 1.2 dynamic_slice.28
  740.8 1.2 dynamic_slice.28
  760.2 1.2 dynamic_slice.28
  774.0 1.2 dynamic_slice.28
  793.4 1.7 bitcast_dynamic-update-slice_fusion
  795.1 1.9 convolution_add_fusion.1
  797.0 2.4 fusion
  799.4 718.7 %all-reduce.2 = bf16[1280,320]{0,1:T(8,128)(2,1)} all-reduce(f32[1280,320]{0,1:T(8,128)S(1)} %convolution_bitcast_fusion), channel_id=1, replica_groups=mesh['tm'=128,'head'=4] {'tm'}, use_global_device_ids=true, to_apply=%region_6.7 | all-reduce | flops 409600 | bytes 2457600 | tf_op jit(solution)/shard_map/psum | solution.py:133
  (325 shorter events, 257.1 us)
Async XLA Ops:
  7.2 25.6 %copy-start = (bf16[1280,320]{0,1:T(8,128)(2,1)S(1)}, bf16[1280,320]{0,1:T(8,128)(2,1)}, u32[]{:S(2)}) copy-start(bf16[1280,320]{0,1:T(8,128)(2,1)} %param.12) | copy-start | bytes 2457604
  7.2 30.3 %copy-start.1 = (bf16[1280,320]{0,1:T(8,128)(2,1)S(1)}, bf16[1280,320]{0,1:T(8,128)(2,1)}, u32[]{:S(2)}) copy-start(bf16[1280,320]{0,1:T(8,128)(2,1)} %param.14) | copy-start | bytes 2457604
  7.2 434.6 %all-gather.5.cloned.1.call-start = ((), (), s32[]{:S(2)}) async-start(), calls=%async_computation.2 | async-start | bytes 6340608 | tf_op jit(solution)/shard_map/all_gather | solution.py:22
  19.7 3.1 collective-permute-start.2
  22.8 11.7 collective-permute-start.4
  27.2 7.3 collective-permute-start.3
  35.6 386.4 %copy-start.6 = (f32[2,5,64]{2,0,1:T(2,128)}, f32[2,5,64]{2,0,1:T(2,128)S(1)}, u32[]{:S(2)}) copy-start(f32[2,5,64]{2,0,1:T(2,128)S(1)} %max.9) | copy-start | bytes 7684
  35.8 387.0 %copy-start.8 = (f32[2,5,64]{2,0,1:T(2,128)}, f32[2,5,64]{2,0,1:T(2,128)S(1)}, u32[]{:S(2)}) copy-start(f32[2,5,64]{2,0,1:T(2,128)S(1)} %add.101) | copy-start | bytes 7684
  37.4 404.4 %all-gather.3.cloned.1.call-start = ((), (), s32[]{:S(2)}) async-start(), calls=%async_computation.1 | async-start | bytes 6340608 | tf_op jit(solution)/shard_map/all_gather | solution.py:22
  38.0 7.2 collective-permute-start
  45.2 9.4 collective-permute-start.5
  49.4 6.9 collective-permute-start.1
  56.5 368.5 %copy-start.4 = (bf16[64,320]{0,1:T(8,128)(2,1)}, bf16[64,320]{0,1:T(8,128)(2,1)S(1)}, u32[]{:S(2)}) copy-start(bf16[64,320]{0,1:T(8,128)(2,1)S(1)} %copy.160) | copy-start | bytes 122884
  56.6 0.7 copy-start.2
  59.2 1460.4 %reduce-scatter.2.cloned.1.call-start = ((), (), s32[]{:S(2)}) async-start(), calls=%async_computation.3 | async-start | bytes 409600 | tf_op jit(solution)/shard_map/reduce_scatter | solution.py:167
  422.8 14.3 collective-permute-start.7
  434.3 1084.1 %copy-start.5 = (bf16[64,320]{0,1:T(8,128)(2,1)S(1)}, bf16[64,320]{0,1:T(8,128)(2,1)}, u32[]{:S(2)}) copy-start(bf16[64,320]{0,1:T(8,128)(2,1)} %copy-done.4) | copy-start | bytes 122884
  434.3 1084.1 %copy-start.7 = (f32[2,5,64]{2,0,1:T(2,128)S(1)}, f32[2,5,64]{2,0,1:T(2,128)}, u32[]{:S(2)}) copy-start(f32[2,5,64]{2,0,1:T(2,128)} %copy-done.6) | copy-start | bytes 7684
  434.3 1084.1 %copy-start.9 = (f32[2,5,64]{2,0,1:T(2,128)S(1)}, f32[2,5,64]{2,0,1:T(2,128)}, u32[]{:S(2)}) copy-start(f32[2,5,64]{2,0,1:T(2,128)} %copy-done.8) | copy-start | bytes 7684
  435.0 6.8 collective-permute-start.6
  795.1 723.1 %copy-start.3 = (bf16[2,64,5,64]{3,2,1,0:T(8,128)(2,1)S(1)}, bf16[2,64,5,64]{3,2,1,0:T(8,128)(2,1)}, u32[]{:S(2)}) copy-start(bf16[2,64,5,64]{3,2,1,0:T(8,128)(2,1)} %copy-done.2) | copy-start | bytes 245764
Sparse Core Ops, SparseCore 0:
  37.6 152.8 all-gather.4
  194.7 142.9 all-gather.2
  799.6 10.8 reduce-scatter.1
where the time goes:
time: 1540 us; the launch traced here: 1530 us
  blocking collectives  1090 us (71%)
  local copies, waits for them, and re-layouts  171 us (11%)
  other arithmetic  117 us (8%)
  loops' own time  86.2 us (6%)
  starting transfers between devices  28.8 us (2%)
    psum x1, blocking collectives, shards(): grad_weight = lax.psum(weight_part, 'tm')  719 us
    unnamed x1, blocking collectives  360 us
    dynamic_slice x127, local copies, waits for them, and re-layouts, one(): lax.dynamic_index_in_dim(a, source, 0, False).astype(own.dtype)  154 us
    add x127, other arithmetic, segment_add(): return (flag, later[1] + keep * earlier[1], later[2] + keep * earlier[2])  111 us
    another operation x1, loops' own time, carried_in(): return lax.fori_loop(0, ahead, one, state)  86.2 us
  transfers between devices with their start and end apart: 11, of which 4 were waited for; matrix products, arithmetic and copies ran while one was open for 2% of the time, Pallas kernels for 0%

commit v1 on v0

v1 whole, which is shorter than its diff:
```python
import functools

import jax
import jax.numpy as jnp
from jax import lax
from jax.experimental import pallas as pl
from jax.experimental.pallas import tpu as pltpu
from jax.sharding import PartitionSpec as P

MESH = pl.DeviceIdType.MESH
F32 = jnp.float32
BF16 = jnp.bfloat16

P_SIZE = 64
HD = 64
SPAN = 4
NZ = 8
GROUP = 8
CROSS = 16
HEADS_AX = 4
WIN = 384
NT = (((1,), (1,)), ((), ()))


def mm(a, b):
    return jnp.dot(a, b, preferred_element_type=F32)


def mm_nt(a, b):
    return lax.dot_general(a, b, NT, preferred_element_type=F32)


def roll_half(x):
    return pltpu.roll(x, P_SIZE, 1)


def low_lanes(shape):
    return lax.broadcasted_iota(jnp.int32, shape, 1) < P_SIZE


def pack(tile, half):
    n = tile.shape[0] // 2
    top, bottom = tile[:n], tile[n:]
    low = low_lanes((n, 128))
    if half == 0:
        return jnp.where(low, top, roll_half(bottom))
    return jnp.where(low, roll_half(top), bottom)


def unpack(first, second):
    low = low_lanes(first.shape)
    return jnp.concatenate(
        [jnp.where(low, first, roll_half(second)), jnp.where(low, roll_half(first), second)], 0
    )


def kernel(
    hid_ref, wq_ref, wk_ref, wv_ref, go_ref,
    att_ref, gw_ref, gh_ref,
    xt, et, wt, gt, pk_lo, pk_hi, in_lo, in_hi,
    qkv, kve, kvn, dqt, fall, dqall, part, parts_in, small, yt, gh_in, pg_lo, pg_hi, gin_lo, gin_hi,
    pts, local_sem, a1_s, a1_r, a2_s, a2_r, a3_s, a3_r, fe_s, fe_r, c_s, c_r,
    e_s, e_r, f_s, f_r, g_s, g_r, h_s, h_r, z_s, z_r,
):
    tm = lax.axis_index("tm")
    head = lax.axis_index("head")
    core = head % 2
    z = tm % NZ
    xh = (tm // NZ) % 2
    y = tm // (2 * NZ)
    place = z % SPAN
    pos = (1 - core) * z + core * y
    stride = (1 - core) + core * 2 * NZ
    pos2 = (1 - core) * y + core * z
    stride2 = (1 - core) * 2 * NZ + core
    cross = pos2 * 2 + xh
    width = hid_ref.shape[0]
    half_w = width // 2

    def copy(src, dst, send, recv, device):
        return pltpu.make_async_remote_copy(
            src_ref=src, dst_ref=dst, send_sem=send, recv_sem=recv,
            device_id=device, device_id_type=MESH,
        )

    def head_peer(r):
        return (tm, (head + r) % HEADS_AX)

    def group_pos(r):
        return (pos + r) % GROUP

    def group_peer(r):
        return (tm + (group_pos(r) - pos) * stride, head)

    def cross_pos(r):
        return (cross + r) % CROSS

    def cross_peer(r):
        k = cross_pos(r)
        return (tm + (k // 2 - pos2) * stride2 + (k % 2 - xh) * NZ, head)

    def head_rows(h):
        return pl.ds(pl.multiple_of(h * width, 64), width)

    def win_start(j):
        a = j // 2
        return pl.multiple_of(640 * (a // 2) + 256 * (a % 2), 128)

    def win_rows(j):
        return pl.multiple_of((j % 2) * half_w, 32)

    own_x = xt.at[head_rows(head)]
    loads = [
        pltpu.make_async_copy(hid_ref, own_x, local_sem.at[0]),
        pltpu.make_async_copy(wq_ref, wt.at[pl.ds(0, width)], local_sem.at[1]),
        pltpu.make_async_copy(wk_ref, wt.at[pl.ds(width, width)], local_sem.at[2]),
        pltpu.make_async_copy(wv_ref, wt.at[pl.ds(2 * width, width)], local_sem.at[3]),
        pltpu.make_async_copy(go_ref, gt, local_sem.at[4]),
    ]
    for load in loads:
        load.start()

    barrier = pltpu.get_barrier_semaphore()
    peers = (
        [head_peer(r) for r in range(1, HEADS_AX)]
        + [group_peer(r) for r in range(1, GROUP)]
        + [cross_peer(r) for r in range(1, CROSS)]
    )
    for peer in peers:
        pl.semaphore_signal(barrier, inc=1, device_id=peer, device_id_type=MESH)
    loads[0].wait()
    tile = xt[head_rows(head), :].astype(F32)
    pk_lo[...] = pack(tile, 0).astype(BF16)
    pk_hi[...] = pack(tile, 1).astype(BF16)
    pl.semaphore_wait(barrier, len(peers))

    def a1(r):
        return copy(own_x, own_x, a1_s.at[r - 1], a1_r.at[r - 1], head_peer(r))

    def a1_in(r):
        rows = xt.at[head_rows((head - r + HEADS_AX) % HEADS_AX)]
        return copy(rows, rows, a1_s.at[r - 1], a1_r.at[r - 1], head_peer(r))

    for r in range(1, HEADS_AX):
        a1(r).start()

    def lead_out(p):
        return copy(pk_lo, in_lo, a2_s.at[p - 1], a2_r.at[0], (tm + p, head))

    def prev_out():
        return copy(pk_hi, in_hi, a2_s.at[3], a2_r.at[1], (tm + 1, head))

    @pl.when(place == 0)
    def _():
        for p in range(1, SPAN):
            lead_out(p).start()

    @pl.when(place < SPAN - 1)
    def _():
        prev_out().start()

    own_e = et.at[head_rows(head)]

    @pl.when(place == 0)
    def _():
        et[head_rows(head), :] = jnp.where(low_lanes(tile.shape), tile, roll_half(tile)).astype(BF16)

    @pl.when(place > 0)
    def _():
        copy(pk_lo, in_lo, a2_s.at[0], a2_r.at[0], (tm, (head + 1) % HEADS_AX)).wait_recv()
        copy(pk_hi, in_hi, a2_s.at[3], a2_r.at[1], (tm, (head + 1) % HEADS_AX)).wait_recv()
        et[head_rows(head), :] = unpack(in_lo[...].astype(F32), in_hi[...].astype(F32)).astype(BF16)

    def a3(r):
        return copy(own_e, own_e, a3_s.at[r - 1], a3_r.at[r - 1], head_peer(r))

    def a3_in(r):
        rows = et.at[head_rows((head - r + HEADS_AX) % HEADS_AX)]
        return copy(rows, rows, a3_s.at[r - 1], a3_r.at[r - 1], head_peer(r))

    for r in range(1, HEADS_AX):
        a3(r).start()
    for r in range(1, HEADS_AX):
        a1_in(r).wait_recv()

    def fe(r):
        return copy(
            xt.at[pl.ds(win_start(group_pos(r)), WIN)], fall.at[:, pl.ds(128 * r, 128)],
            fe_s.at[r - 1], fe_r.at[r - 1], group_peer(r),
        )

    for r in range(1, GROUP):
        fe(r).start()
    fall[:, 0:128] = xt[pl.ds(win_start(pos), WIN), :]

    for load in loads[1:]:
        load.wait()
    qkv[...] = mm(wt[...], xt[...]).astype(BF16)
    kvn[1] = jnp.transpose(qkv[width:, :])
    for r in range(1, HEADS_AX):
        a3_in(r).wait_recv()
    kve[...] = mm(wt[width:, :], et[...]).astype(BF16)
    kvn[0] = jnp.transpose(kve[...])

    scale = HD ** (-0.5)
    low = low_lanes((P_SIZE, 128))
    zero = jnp.zeros((P_SIZE, 128), BF16)
    heads_here = width // HD

    def spread(lead, second, index):
        pts[index, 0:64, :] = lead
        pts[index, 64:128, :] = jnp.where(low, second, zero)
        pts[index, 128:192, :] = jnp.where(low, zero, second)
        pts[index, 192:256, :] = zero

    for i in range(heads_here):
        a, b = HD * i, HD * (i + 1)
        q = qkv[a:b, :]
        cot = gt[a:b, :]
        k_extra, k_own = kvn[0, :, a:b], kvn[1, 0:64, a:b]
        v_extra, v_own = kvn[0, :, width + a : width + b], kvn[1, 0:64, width + a : width + b]
        s_extra, s_own = mm(k_extra, q) * scale, mm(k_own, q) * scale
        s_lead, s_second = s_extra[:64], jnp.where(low, s_extra[64:], s_own)
        top = jnp.maximum(
            jnp.max(s_lead, 0, keepdims=True), jnp.max(s_second, 0, keepdims=True)
        )
        e_lead, e_second = jnp.exp(s_lead - top), jnp.exp(s_second - top)
        inv = 1.0 / (jnp.sum(e_lead, 0, keepdims=True) + jnp.sum(e_second, 0, keepdims=True))
        p_lead, p_second = e_lead * inv, e_second * inv
        d_extra, d_own = mm(v_extra, cot), mm(v_own, cot)
        d_lead, d_second = d_extra[:64], jnp.where(low, d_extra[64:], d_own)
        inner = jnp.sum(p_lead * d_lead, 0, keepdims=True) + jnp.sum(
            p_second * d_second, 0, keepdims=True
        )
        spread(
            (p_lead * (d_lead - inner) * scale).astype(BF16),
            (p_second * (d_second - inner) * scale).astype(BF16),
            2 * i,
        )
        spread(p_lead.astype(BF16), p_second.astype(BF16), 2 * i + 1)
        k_wide = jnp.concatenate([kve[a:b, :], qkv[width + a : width + b, :]], 1)
        dqt[a:b, :] = mm(k_wide, pts[2 * i]).astype(BF16)

    def cc(r):
        return copy(
            dqt.at[pl.ds(win_rows(group_pos(r)), half_w)], dqall.at[:, pl.ds(128 * r, 128)],
            c_s.at[r - 1], c_r.at[r - 1], group_peer(r),
        )

    for r in range(1, GROUP):
        cc(r).start()
    dqall[:, 0:128] = dqt[pl.ds(win_rows(pos), half_w), :]

    dks, dvs = [], []
    for i in range(heads_here):
        a, b = HD * i, HD * (i + 1)
        v_wide = jnp.concatenate(
            [kve[width + a : width + b, :], qkv[2 * width + a : 2 * width + b, :]], 1
        )
        att_ref[a:b, :] = mm(v_wide, pts[2 * i + 1]).astype(BF16)
        dks.append(mm_nt(qkv[a:b, :], pts[2 * i]).astype(BF16))
        dvs.append(mm_nt(gt[a:b, :], pts[2 * i + 1]).astype(BF16))

    dk_n = jnp.transpose(jnp.concatenate(dks, 0))
    dv_n = jnp.transpose(jnp.concatenate(dvs, 0))
    dq_n = jnp.transpose(dqt[...])
    for c in range(5):
        cols = slice(256 * c, 256 * (c + 1))
        terms = mm(dk_n, wt[width : 2 * width, cols]) + mm(dv_n, wt[2 * width :, cols])
        own = terms[128:] + mm(dq_n, wt[0:width, cols])
        yt[cols, 0:128] = jnp.transpose(terms[:128].astype(BF16))
        yt[cols, 128:256] = jnp.transpose(own.astype(BF16))

    def hh(r):
        return copy(
            yt.at[head_rows((head + r) % HEADS_AX)], gh_in.at[r - 1],
            h_s.at[r - 1], h_r.at[r - 1], head_peer(r),
        )

    for r in range(1, HEADS_AX):
        hh(r).start()

    for r in range(1, GROUP):
        fe(r).wait_recv()
    for r in range(1, GROUP):
        cc(r).wait_recv()
    window = mm_nt(dqall[...], fall[...]).astype(BF16)
    for k in range(15):
        i, l = k // 3, k % 3
        part[k] = window[32 * i : 32 * i + 32, 128 * l : 128 * l + 128]
    part[15] = jnp.zeros((32, 128), BF16)

    def ee(r):
        return copy(
            part.at[cross_pos(r)], parts_in.at[r - 1], e_s.at[r - 1], e_r.at[r - 1], cross_peer(r)
        )

    for r in range(1, CROSS):
        ee(r).start()
    for r in range(1, CROSS):
        ee(r).wait_recv()
    total = part[cross].astype(F32)
    for r in range(1, CROSS):
        total = total + parts_in[r - 1].astype(F32)

    even = (pos // 2) % 2 == 0

    def piece(k):
        return gw_ref.at[
            pl.ds(pl.multiple_of(win_rows(pos) + 32 * (k // 3), 32), 32),
            pl.ds(pl.multiple_of(win_start(pos) + 128 * (k % 3), 128), 128),
        ]

    def holds(k):
        return (k < 15) & (even | (k % 3 > 0))

    def ff(r):
        return copy(piece(cross), piece(cross), f_s.at[r - 1], f_r.at[r - 1], cross_peer(r))

    def ff_in(r):
        k = (cross - r + CROSS) % CROSS
        return k, copy(piece(k), piece(k), f_s.at[r - 1], f_r.at[r - 1], cross_peer(r))

    @pl.when(holds(cross))
    def _():
        gw_ref[
            pl.ds(pl.multiple_of(win_rows(pos) + 32 * (cross // 3), 32), 32),
            pl.ds(pl.multiple_of(win_start(pos) + 128 * (cross % 3), 128), 128),
        ] = total.astype(BF16)
        for r in range(1, CROSS):
            ff(r).start()

    for r in range(1, HEADS_AX):
        hh(r).wait_recv()
    summed = yt[head_rows(head), :].astype(F32)
    for r in range(1, HEADS_AX):
        summed = summed + gh_in[r - 1].astype(F32)
    extra, own = summed[:, :128], summed[:, 128:]
    pg_lo[...] = pack(extra, 0).astype(BF16)
    pg_hi[...] = pack(extra, 1).astype(BF16)

    def lead_back(p):
        return copy(pg_lo, gin_lo.at[p - 1], z_s.at[0], z_r.at[p - 1], (tm - p, head))

    def prev_back():
        return copy(pg_hi, gin_hi, z_s.at[1], z_r.at[3], (tm - 1, head))

    for p in range(1, SPAN):
        @pl.when(place == p)
        def _(p=p):
            lead_back(p).start()
            prev_back().start()

    for r in range(1, CROSS):
        k, arrival = ff_in(r)

        @pl.when(holds(k))
        def _(arrival=arrival):
            arrival.wait_recv()

    def wide(j):
        return gw_ref.at[
            pl.ds(win_rows(j), half_w), pl.ds(pl.multiple_of(win_start(j) + 128, 128), 256)
        ]

    def slim(j):
        return gw_ref.at[pl.ds(win_rows(j), half_w), pl.ds(win_start(j), 128)]

    def gg(r, j, region, slot):
        return copy(
            region(j), region(j), g_s.at[slot, r - 1], g_r.at[slot, r - 1], group_peer(r)
        )

    for r in range(1, GROUP):
        gg(r, pos, wide, 0).start()

        @pl.when(even)
        def _(r=r):
            gg(r, pos, slim, 1).start()

    low_tile = low_lanes(own.shape)

    @pl.when(place == 0)
    def _():
        for p in range(1, SPAN):
            copy(pg_lo, gin_lo.at[p - 1], z_s.at[0], z_r.at[p - 1], (tm, (head + 1) % HEADS_AX)).wait_recv()

    @pl.when(place < SPAN - 1)
    def _():
        copy(pg_hi, gin_hi, z_s.at[1], z_r.at[3], (tm, (head + 1) % HEADS_AX)).wait_recv()

    lead_sum = gin_lo[0].astype(F32) + gin_lo[1].astype(F32) + gin_lo[2].astype(F32)
    lead_sum = jnp.where(place == 0, lead_sum, 0.0)
    prev_in = jnp.where(place < SPAN - 1, gin_hi[...].astype(F32), 0.0)
    local = jnp.where((place == 0) & low_tile, extra + roll_half(extra), 0.0)
    gh_ref[...] = (own + local + unpack(lead_sum, prev_in)).astype(BF16)

    for r in range(1, GROUP):
        j = (pos - r + GROUP) % GROUP
        gg(r, j, wide, 0).wait_recv()

        @pl.when((j // 2) % 2 == 0)
        def _(r=r, j=j):
            gg(r, j, slim, 1).wait_recv()

    for r in range(1, HEADS_AX):
        a1(r).wait_send()
        a3(r).wait_send()
        hh(r).wait_send()

    @pl.when(place == 0)
    def _():
        for p in range(1, SPAN):
            lead_out(p).wait_send()

    @pl.when(place < SPAN - 1)
    def _():
        prev_out().wait_send()

    @pl.when(place > 0)
    def _():
        lead_back(1).wait_send()
        prev_back().wait_send()

    for r in range(1, GROUP):
        fe(r).wait_send()
        cc(r).wait_send()
        gg(r, pos, wide, 0).wait_send()

    @pl.when(even)
    def _():
        for r in range(1, GROUP):
            gg(r, pos, slim, 1).wait_send()

    for r in range(1, CROSS):
        ee(r).wait_send()

    @pl.when(holds(cross))
    def _():
        for r in range(1, CROSS):
            ff(r).wait_send()


def shards(hidden_states, w_query, w_key, w_value, grad_out):
    rows, width = hidden_states.shape
    full = w_query.shape[0]
    half = width // 2
    vm = pltpu.VMEM
    dma = pltpu.SemaphoreType.DMA
    scratch = [
        vm((full, rows), BF16),
        vm((full, rows), BF16),
        vm((3 * width, full), BF16),
        vm((width, rows), BF16),
        vm((half, 128), BF16), vm((half, 128), BF16),
        vm((half, 128), BF16), vm((half, 128), BF16),
        vm((3 * width, rows), BF16),
        vm((2 * width, rows), BF16),
        vm((2, rows, 2 * width), BF16),
        vm((width, rows), BF16),
        vm((WIN, GROUP * 128), BF16),
        vm((half, GROUP * 128), BF16),
        vm((CROSS, 32, 128), BF16),
        vm((CROSS - 1, 32, 128), BF16),
        vm((8, 128), F32),
        vm((full, 256), BF16),
        vm((HEADS_AX - 1, width, 256), BF16),
        vm((half, 128), BF16), vm((half, 128), BF16),
        vm((SPAN - 1, half, 128), BF16), vm((half, 128), BF16),
        vm((2 * (width // HD), 256, 128), BF16),
        dma((5,)),
        dma((3,)), dma((3,)),
        dma((4,)), dma((2,)),
        dma((3,)), dma((3,)),
        dma((GROUP - 1,)), dma((GROUP - 1,)),
        dma((GROUP - 1,)), dma((GROUP - 1,)),
        dma((CROSS - 1,)), dma((CROSS - 1,)),
        dma((CROSS - 1,)), dma((CROSS - 1,)),
        dma((2, GROUP - 1)), dma((2, GROUP - 1)),
        dma((3,)), dma((3,)),
        dma((2,)), dma((4,)),
    ]
    att, gw, gh = pl.pallas_call(
        kernel,
        out_shape=(
            jax.ShapeDtypeStruct((width, rows), BF16),
            jax.ShapeDtypeStruct((width, full), BF16),
            jax.ShapeDtypeStruct((width, rows), BF16),
        ),
        in_specs=[pl.BlockSpec(memory_space=pl.ANY)] * 5,
        out_specs=[pl.BlockSpec(memory_space=pltpu.VMEM)] * 3,
        scratch_shapes=scratch,
        compiler_params=pltpu.CompilerParams(
            collective_id=0, has_side_effects=True, vmem_limit_bytes=40 * 2**20
        ),
    )(hidden_states.T, w_query.T, w_key.T, w_value.T, grad_out.T)
    return att.T, gw.T, gh.T


def solution(mesh):
    placed = (P("tm", "head"), P(None, "head"), P(None, "head"), P(None, "head"), P("tm", "head"))
    return jax.shard_map(
        shards,
        mesh=mesh,
        in_specs=placed,
        out_specs=(P("tm", "head"), P(None, "head"), P("tm", "head")),
        check_vma=False,
    )
```

time: 1540 us -> 72.6 us (0.05)
  the two profiles are of different devices: /device:TPU:2 before, /device:TPU:1 now
where the time goes in v1:
time: 72.6 us; the launch traced here: 72.3 us
  Pallas kernels  64.2 us (88%)
  local copies, waits for them, and re-layouts  7.36 us (10%)
    pallas_call x1, Pallas kernels, shards(): pl.pallas_call(kernel, out_shape=(jax.ShapeDtypeStruct((width, rows), BF1...  64.2 us
    unnamed x13, local copies, waits for them, and re-layouts  7.36 us

profile of v1, /device:TPU:1, one launch (start us, length us, event | category | flops | bytes accessed | tf_op | source)
XLA Modules:
  0.0 72.3 jit_solution(16727221611009369345)
XLA Ops:
  0.6 0.0 copy-start
  0.6 1.1 %copy-done = bf16[1280,320]{0,1:T(8,128)(2,1)S(1)} copy-done((bf16[1280,320]{0,1:T(8,128)(2,1)S(1)}, bf16[1280,320]{0,1:T(8,128)(2,1)}, u32[]{:S(2)}) %copy-start) | copy-done | bytes 819224
  1.8 0.0 copy-start.1
  1.8 1.1 %copy-done.1 = bf16[1280,320]{0,1:T(8,128)(2,1)S(1)} copy-done((bf16[1280,320]{0,1:T(8,128)(2,1)S(1)}, bf16[1280,320]{0,1:T(8,128)(2,1)}, u32[]{:S(2)}) %copy-start.1) | copy-done | bytes 819224
  2.9 0.0 copy-start.2
  2.9 1.1 %copy-done.2 = bf16[1280,320]{0,1:T(8,128)(2,1)S(1)} copy-done((bf16[1280,320]{0,1:T(8,128)(2,1)S(1)}, bf16[1280,320]{0,1:T(8,128)(2,1)}, u32[]{:S(2)}) %copy-start.2) | copy-done | bytes 819224
  4.1 0.0 copy-start.3
  4.1 0.9 %copy-done.3 = bf16[128,320]{0,1:T(8,128)(2,1)S(1)} copy-done((bf16[128,320]{0,1:T(8,128)(2,1)S(1)}, bf16[128,320]{0,1:T(8,128)(2,1)}, u32[]{:S(2)}) %copy-start.3) | copy-done | bytes 81944
  5.0 0.0 copy-start.4
  5.0 0.9 %copy-done.4 = bf16[128,320]{0,1:T(8,128)(2,1)S(1)} copy-done((bf16[128,320]{0,1:T(8,128)(2,1)S(1)}, bf16[128,320]{0,1:T(8,128)(2,1)}, u32[]{:S(2)}) %copy-start.4) | copy-done | bytes 81944
  5.8 64.2 %shard_map.76 = (bf16[320,128]{1,0:T(8,128)(2,1)S(1)}, bf16[320,1280]{1,0:T(8,128)(2,1)S(1)}, bf16[320,128]{1,0:T(8,128)(2,1)S(1)}) custom-call(bf16[320,128]{1,0:T(8,128)(2,1)S(1)} %bitcast.12, bf16[320,1280]{1,0:T(8,128)(2,1)S(1)} %bitcast.8, bf16[320,1280]{1,0:T(8,128)(2,1)S(1)} %bitcast.9, bf16[320,1280]{1,0:T(8,128)(2,1)S(1)} %bitcast.10, ...), custom_call_target="tpu_custom_call" | custom-call | tf_op jit(solution)/shard_map/pallas_call | solution.py:483
  70.1 0.6 copy.11
  70.7 0.9 %copy.12 = bf16[1280,320]{0,1:T(8,128)(2,1)} copy(bf16[1280,320]{0,1:T(8,128)(2,1)S(1)} %bitcast.11) | data formatting | bytes 1638400
  71.6 0.6 copy.13
Async XLA Ops:
  0.6 1.1 %copy-start = (bf16[1280,320]{0,1:T(8,128)(2,1)S(1)}, bf16[1280,320]{0,1:T(8,128)(2,1)}, u32[]{:S(2)}) copy-start(bf16[1280,320]{0,1:T(8,128)(2,1)} %param.6) | copy-start | bytes 2457604
  1.8 1.1 %copy-start.1 = (bf16[1280,320]{0,1:T(8,128)(2,1)S(1)}, bf16[1280,320]{0,1:T(8,128)(2,1)}, u32[]{:S(2)}) copy-start(bf16[1280,320]{0,1:T(8,128)(2,1)} %param.7) | copy-start | bytes 2457604
  2.9 1.1 %copy-start.2 = (bf16[1280,320]{0,1:T(8,128)(2,1)S(1)}, bf16[1280,320]{0,1:T(8,128)(2,1)}, u32[]{:S(2)}) copy-start(bf16[1280,320]{0,1:T(8,128)(2,1)} %param.8) | copy-start | bytes 2457604
  4.1 0.9 %copy-start.3 = (bf16[128,320]{0,1:T(8,128)(2,1)S(1)}, bf16[128,320]{0,1:T(8,128)(2,1)}, u32[]{:S(2)}) copy-start(bf16[128,320]{0,1:T(8,128)(2,1)} %param.5) | copy-start | bytes 245764
  5.0 0.9 %copy-start.4 = (bf16[128,320]{0,1:T(8,128)(2,1)S(1)}, bf16[128,320]{0,1:T(8,128)(2,1)}, u32[]{:S(2)}) copy-start(bf16[128,320]{0,1:T(8,128)(2,1)} %param.9) | copy-start | bytes 245764

commit v2 on v1

--- a/solution.py
+++ b/solution.py
@@ -18,6 +18,8 @@
 GROUP = 8
 CROSS = 16
 HEADS_AX = 4
+FAR_FIRST = sorted(range(1, GROUP), key=lambda r: abs(r - GROUP // 2))
+CROSS_FAR_FIRST = sorted(range(1, CROSS), key=lambda r: abs(r - CROSS // 2))
 WIN = 384
 NT = (((1,), (1,)), ((), ()))
 
@@ -58,7 +60,7 @@
     hid_ref, wq_ref, wk_ref, wv_ref, go_ref,
     att_ref, gw_ref, gh_ref,
     xt, et, wt, gt, pk_lo, pk_hi, in_lo, in_hi,
-    qkv, kve, kvn, dqt, fall, dqall, part, parts_in, small, yt, gh_in, pg_lo, pg_hi, gin_lo, gin_hi,
+    qkv, kve, kvn, dqt, fall, dqall, part, parts_in, yt, gh_in, pg_lo, pg_hi, gin_lo, gin_hi,
     pts, local_sem, a1_s, a1_r, a2_s, a2_r, a3_s, a3_r, fe_s, fe_r, c_s, c_r,
     e_s, e_r, f_s, f_r, g_s, g_r, h_s, h_r, z_s, z_r,
 ):
@@ -102,12 +104,28 @@
     def head_rows(h):
         return pl.ds(pl.multiple_of(h * width, 64), width)
 
+    def is_wide(j):
+        return (j // 2) % 2 == 0
+
+    def by_tiles(j, run):
+        pl.when(is_wide(j))(lambda: run(3))
+        pl.when(jnp.logical_not(is_wide(j)))(lambda: run(2))
+
     def win_start(j):
         a = j // 2
-        return pl.multiple_of(640 * (a // 2) + 256 * (a % 2), 128)
+        return pl.multiple_of(640 * (a // 2) + 384 * (a % 2), 128)
 
     def win_rows(j):
         return pl.multiple_of((j % 2) * half_w, 32)
+
+    barrier = pltpu.get_barrier_semaphore()
+    peers = (
+        [head_peer(r) for r in range(1, HEADS_AX)]
+        + [group_peer(r) for r in range(1, GROUP)]
+        + [cross_peer(r) for r in range(1, CROSS)]
+    )
+    for peer in peers:
+        pl.semaphore_signal(barrier, inc=1, device_id=peer, device_id_type=MESH)
 
     own_x = xt.at[head_rows(head)]
     loads = [
@@ -119,15 +137,6 @@
     ]
     for load in loads:
         load.start()
-
-    barrier = pltpu.get_barrier_semaphore()
-    peers = (
-        [head_peer(r) for r in range(1, HEADS_AX)]
-        + [group_peer(r) for r in range(1, GROUP)]
-        + [cross_peer(r) for r in range(1, CROSS)]
-    )
-    for peer in peers:
-        pl.semaphore_signal(barrier, inc=1, device_id=peer, device_id_type=MESH)
     loads[0].wait()
     tile = xt[head_rows(head), :].astype(F32)
     pk_lo[...] = pack(tile, 0).astype(BF16)
@@ -183,15 +192,24 @@
     for r in range(1, HEADS_AX):
         a1_in(r).wait_recv()
 
-    def fe(r):
+    def fe(r, j, tiles):
         return copy(
-            xt.at[pl.ds(win_start(group_pos(r)), WIN)], fall.at[:, pl.ds(128 * r, 128)],
+            xt.at[pl.ds(win_start(j), 128 * tiles)], fall.at[r, pl.ds(0, 128 * tiles)],
             fe_s.at[r - 1], fe_r.at[r - 1], group_peer(r),
         )
 
-    for r in range(1, GROUP):
-        fe(r).start()
-    fall[:, 0:128] = xt[pl.ds(win_start(pos), WIN), :]
+    for r in FAR_FIRST:
+        by_tiles(group_pos(r), lambda tiles, r=r: fe(r, group_pos(r), tiles).start())
+
+    @pl.when(is_wide(pos))
+    def _():
+        fall[0] = xt[pl.ds(win_start(pos), 384), :]
+
+    @pl.when(jnp.logical_not(is_wide(pos)))
+    def _():
+        fall[0, 0:256] = xt[pl.ds(win_start(pos), 256), :]
+        for r in range(GROUP):
+            fall[r, 256:384] = jnp.zeros((128, 128), BF16)
 
     for load in loads[1:]:
         load.wait()
@@ -212,6 +230,16 @@
         pts[index, 64:128, :] = jnp.where(low, second, zero)
         pts[index, 128:192, :] = jnp.where(low, zero, second)
         pts[index, 192:256, :] = zero
+
+    def cc(r):
+        return copy(
+            dqt.at[pl.ds(win_rows(group_pos(r)), half_w)], dqall.at[r],
+            c_s.at[r - 1], c_r.at[r - 1], group_peer(r),
+        )
+
+    def send_half(part):
+        for r in FAR_FIRST:
+            pl.when(group_pos(r) % 2 == part)(lambda r=r: cc(r).start())
 
     for i in range(heads_here):
         a, b = HD * i, HD * (i + 1)
@@ -240,16 +268,11 @@
         spread(p_lead.astype(BF16), p_second.astype(BF16), 2 * i + 1)
         k_wide = jnp.concatenate([kve[a:b, :], qkv[width + a : width + b, :]], 1)
         dqt[a:b, :] = mm(k_wide, pts[2 * i]).astype(BF16)
-
-    def cc(r):
-        return copy(
-            dqt.at[pl.ds(win_rows(group_pos(r)), half_w)], dqall.at[:, pl.ds(128 * r, 128)],
-            c_s.at[r - 1], c_r.at[r - 1], group_peer(r),
-        )
-
-    for r in range(1, GROUP):
-        cc(r).start()
-    dqall[:, 0:128] = dqt[pl.ds(win_rows(pos), half_w), :]
+        if a < half_w <= b:
+            send_half(0)
+    send_half(1)
+    dqall[0] = dqt[pl.ds(win_rows(pos), half_w), :]
+
 
     dks, dvs = [], []
     for i in range(heads_here):
@@ -261,30 +284,14 @@
         dks.append(mm_nt(qkv[a:b, :], pts[2 * i]).astype(BF16))
         dvs.append(mm_nt(gt[a:b, :], pts[2 * i + 1]).astype(BF16))
 
-    dk_n = jnp.transpose(jnp.concatenate(dks, 0))
-    dv_n = jnp.transpose(jnp.concatenate(dvs, 0))
-    dq_n = jnp.transpose(dqt[...])
-    for c in range(5):
-        cols = slice(256 * c, 256 * (c + 1))
-        terms = mm(dk_n, wt[width : 2 * width, cols]) + mm(dv_n, wt[2 * width :, cols])
-        own = terms[128:] + mm(dq_n, wt[0:width, cols])
-        yt[cols, 0:128] = jnp.transpose(terms[:128].astype(BF16))
-        yt[cols, 128:256] = jnp.transpose(own.astype(BF16))
-
-    def hh(r):
-        return copy(
-            yt.at[head_rows((head + r) % HEADS_AX)], gh_in.at[r - 1],
-            h_s.at[r - 1], h_r.at[r - 1], head_peer(r),
-        )
-
-    for r in range(1, HEADS_AX):
-        hh(r).start()
-
     for r in range(1, GROUP):
-        fe(r).wait_recv()
+        by_tiles(pos, lambda tiles, r=r: fe(r, pos, tiles).wait_recv())
     for r in range(1, GROUP):
         cc(r).wait_recv()
-    window = mm_nt(dqall[...], fall[...]).astype(BF16)
+    window = mm_nt(
+        jnp.concatenate([dqall[r] for r in range(GROUP)], 1),
+        jnp.concatenate([fall[r] for r in range(GROUP)], 1),
+    ).astype(BF16)
     for k in range(15):
         i, l = k // 3, k % 3
         part[k] = window[32 * i : 32 * i + 32, 128 * l : 128 * l + 128]
@@ -295,16 +302,31 @@
             part.at[cross_pos(r)], parts_in.at[r - 1], e_s.at[r - 1], e_r.at[r - 1], cross_peer(r)
         )
 
-    for r in range(1, CROSS):
+    for r in CROSS_FAR_FIRST:
         ee(r).start()
+
+    dk_n = jnp.transpose(jnp.concatenate(dks, 0))
+    dv_n = jnp.transpose(jnp.concatenate(dvs, 0))
+    dq_n = jnp.transpose(dqt[...])
+
+    def hh(r, part):
+        return copy(
+            yt.at[part, head_rows((head + r) % HEADS_AX)], gh_in.at[part, r - 1],
+            h_s.at[part, r - 1], h_r.at[part, r - 1], head_peer(r),
+        )
+
+    for c in range(5):
+        cols = slice(256 * c, 256 * (c + 1))
+        terms = mm(dk_n[:128], wt[width : 2 * width, cols]) + mm(dv_n[:128], wt[2 * width :, cols])
+        yt[0, cols, :] = jnp.transpose(terms.astype(BF16))
+    for r in range(1, HEADS_AX):
+        hh(r, 0).start()
     for r in range(1, CROSS):
         ee(r).wait_recv()
     total = part[cross].astype(F32)
     for r in range(1, CROSS):
         total = total + parts_in[r - 1].astype(F32)
 
-    even = (pos // 2) % 2 == 0
-
     def piece(k):
         return gw_ref.at[
             pl.ds(pl.multiple_of(win_rows(pos) + 32 * (k // 3), 32), 32),
@@ -312,7 +334,7 @@
         ]
 
     def holds(k):
-        return (k < 15) & (even | (k % 3 > 0))
+        return (k < 15) & (is_wide(pos) | (k % 3 < 2))
 
     def ff(r):
         return copy(piece(cross), piece(cross), f_s.at[r - 1], f_r.at[r - 1], cross_peer(r))
@@ -327,15 +349,21 @@
             pl.ds(pl.multiple_of(win_rows(pos) + 32 * (cross // 3), 32), 32),
             pl.ds(pl.multiple_of(win_start(pos) + 128 * (cross % 3), 128), 128),
         ] = total.astype(BF16)
-        for r in range(1, CROSS):
+        for r in CROSS_FAR_FIRST:
             ff(r).start()
 
-    for r in range(1, HEADS_AX):
-        hh(r).wait_recv()
-    summed = yt[head_rows(head), :].astype(F32)
-    for r in range(1, HEADS_AX):
-        summed = summed + gh_in[r - 1].astype(F32)
-    extra, own = summed[:, :128], summed[:, 128:]
+    for c in range(5):
+        cols = slice(256 * c, 256 * (c + 1))
+        terms = mm(dk_n[128:], wt[width : 2 * width, cols]) + mm(dv_n[128:], wt[2 * width :, cols])
+        terms = terms + mm(dq_n, wt[0:width, cols])
+        yt[1, cols, :] = jnp.transpose(terms.astype(BF16))
+    for r in range(1, HEADS_AX):
+        hh(r, 1).start()
+    for r in range(1, HEADS_AX):
+        hh(r, 0).wait_recv()
+    extra = yt[0, head_rows(head), :].astype(F32)
+    for r in range(1, HEADS_AX):
+        extra = extra + gh_in[0, r - 1].astype(F32)
     pg_lo[...] = pack(extra, 0).astype(BF16)
     pg_hi[...] = pack(extra, 1).astype(BF16)
 
@@ -358,55 +386,77 @@
         def _(arrival=arrival):
             arrival.wait_recv()
 
-    def wide(j):
+    def region(j, tiles, first=0, rows=half_w):
         return gw_ref.at[
-            pl.ds(win_rows(j), half_w), pl.ds(pl.multiple_of(win_start(j) + 128, 128), 256)
+            pl.ds(pl.multiple_of(win_rows(j) + first, 16), rows), pl.ds(win_start(j), 128 * tiles)
         ]
 
-    def slim(j):
-        return gw_ref.at[pl.ds(win_rows(j), half_w), pl.ds(win_start(j), 128)]
-
-    def gg(r, j, region, slot):
-        return copy(
-            region(j), region(j), g_s.at[slot, r - 1], g_r.at[slot, r - 1], group_peer(r)
-        )
-
-    for r in range(1, GROUP):
-        gg(r, pos, wide, 0).start()
-
-        @pl.when(even)
-        def _(r=r):
-            gg(r, pos, slim, 1).start()
-
-    low_tile = low_lanes(own.shape)
+    def at(d):
+        return (pos + d + GROUP) % GROUP
+
+    def peer_at(d):
+        return (tm + (at(d) - pos) * stride, head)
+
+    def hop(slot, j, d, tiles, first=0, rows=half_w):
+        ref = region(j, tiles, first, rows)
+        return copy(ref, ref, g_s.at[slot], g_r.at[slot], peer_at(d))
+
+    near = ((0, 2), (1, -2), (2, 1), (3, -1))
+    onward = (
+        (4, -2, 1, 0, half_w), (5, 2, -1, 0, half_w),
+        (6, -2, 2, 0, half_w // 2), (7, 2, -2, half_w // 2, half_w // 2),
+    )
+    for slot, d in near:
+        by_tiles(pos, lambda tiles, slot=slot, d=d: hop(slot, pos, d, tiles).start())
+    for slot, d in near[:2]:
+        by_tiles(at(-d), lambda tiles, slot=slot, d=d: hop(slot, at(-d), d, tiles).wait_recv())
+        for out, of, dist, first, rows in onward:
+            if of == -d:
+                by_tiles(
+                    at(of),
+                    lambda tiles, out=out, of=of, dist=dist, first=first, rows=rows: hop(
+                        out, at(of), dist, tiles, first, rows
+                    ).start(),
+                )
+
+    for r in range(1, HEADS_AX):
+        hh(r, 1).wait_recv()
+    own = yt[1, head_rows(head), :].astype(F32)
+    for r in range(1, HEADS_AX):
+        own = own + gh_in[1, r - 1].astype(F32)
 
     @pl.when(place == 0)
     def _():
         for p in range(1, SPAN):
-            copy(pg_lo, gin_lo.at[p - 1], z_s.at[0], z_r.at[p - 1], (tm, (head + 1) % HEADS_AX)).wait_recv()
+            copy(
+                pg_lo, gin_lo.at[p - 1], z_s.at[0], z_r.at[p - 1], head_peer(1)
+            ).wait_recv()
 
     @pl.when(place < SPAN - 1)
     def _():
-        copy(pg_hi, gin_hi, z_s.at[1], z_r.at[3], (tm, (head + 1) % HEADS_AX)).wait_recv()
+        copy(pg_hi, gin_hi, z_s.at[1], z_r.at[3], head_peer(1)).wait_recv()
 
     lead_sum = gin_lo[0].astype(F32) + gin_lo[1].astype(F32) + gin_lo[2].astype(F32)
     lead_sum = jnp.where(place == 0, lead_sum, 0.0)
     prev_in = jnp.where(place < SPAN - 1, gin_hi[...].astype(F32), 0.0)
-    local = jnp.where((place == 0) & low_tile, extra + roll_half(extra), 0.0)
+    local = jnp.where((place == 0) & low_lanes(own.shape), extra + roll_half(extra), 0.0)
     gh_ref[...] = (own + local + unpack(lead_sum, prev_in)).astype(BF16)
 
-    for r in range(1, GROUP):
-        j = (pos - r + GROUP) % GROUP
-        gg(r, j, wide, 0).wait_recv()
-
-        @pl.when((j // 2) % 2 == 0)
-        def _(r=r, j=j):
-            gg(r, j, slim, 1).wait_recv()
+    for slot, d in near[2:]:
+        by_tiles(at(-d), lambda tiles, slot=slot, d=d: hop(slot, at(-d), d, tiles).wait_recv())
+    for out, of, dist, first, rows in onward:
+        by_tiles(
+            at(of - dist),
+            lambda tiles, out=out, of=of, dist=dist, first=first, rows=rows: hop(
+                out, at(of - dist), dist, tiles, first, rows
+            ).wait_recv(),
+        )
 
     for r in range(1, HEADS_AX):
         a1(r).wait_send()
         a3(r).wait_send()
-        hh(r).wait_send()
+        hh(r, 0).wait_send()
+        hh(r, 1).wait_send()
 
     @pl.when(place == 0)
     def _():
@@ -423,15 +473,17 @@
         prev_back().wait_send()
 
     for r in range(1, GROUP):
-        fe(r).wait_send()
+        by_tiles(group_pos(r), lambda tiles, r=r: fe(r, group_pos(r), tiles).wait_send())
         cc(r).wait_send()
-        gg(r, pos, wide, 0).wait_send()
-
-    @pl.when(even)
-    def _():
-        for r in range(1, GROUP):
-            gg(r, pos, slim, 1).wait_send()
-
+    for slot, d in near:
+        by_tiles(pos, lambda tiles, slot=slot, d=d: hop(slot, pos, d, tiles).wait_send())
+    for out, of, dist, first, rows in onward:
+        by_tiles(
+            at(of),
+            lambda tiles, out=out, of=of, dist=dist, first=first, rows=rows: hop(
+                out, at(of), dist, tiles, first, rows
+            ).wait_send(),
+        )
     for r in range(1, CROSS):
         ee(r).wait_send()
 
@@ -439,6 +491,22 @@
     def _():
         for r in range(1, CROSS):
             ff(r).wait_send()
+
+
+def hand_out(*refs):
+    count = 3
+    arrays, outs, held, sem = refs[:count], refs[count : 2 * count], refs[2 * count : -1], refs[-1]
+    arrivals = [
+        pltpu.make_async_copy(arrays[i], held[i], sem.at[0, i]) for i in range(count)
+    ]
+    copies = [pltpu.make_async_copy(held[i], outs[i], sem.at[1, i]) for i in range(count)]
+    for arrival in arrivals:
+        arrival.start()
+    for arrival, out in zip(arrivals, copies):
+        arrival.wait()
+        out.start()
+    for out in copies:
+        out.wait()
 
 
 def shards(hidden_states, w_query, w_key, w_value, grad_out):
@@ -458,13 +526,12 @@
         vm((2 * width, rows), BF16),
         vm((2, rows, 2 * width), BF16),
         vm((width, rows), BF16),
-        vm((WIN, GROUP * 128), BF16),
-        vm((half, GROUP * 128), BF16),
+        vm((GROUP, WIN, 128), BF16),
+        vm((GROUP, half, 128), BF16),
         vm((CROSS, 32, 128), BF16),
         vm((CROSS - 1, 32, 128), BF16),
-        vm((8, 128), F32),
-        vm((full, 256), BF16),
-        vm((HEADS_AX - 1, width, 256), BF16),
+        vm((2, full, 128), BF16),
+        vm((2, HEADS_AX - 1, width, 128), BF16),
         vm((half, 128), BF16), vm((half, 128), BF16),
         vm((SPAN - 1, half, 128), BF16), vm((half, 128), BF16),
         vm((2 * (width // HD), 256, 128), BF16),
@@ -476,8 +543,8 @@
         dma((GROUP - 1,)), dma((GROUP - 1,)),
         dma((CROSS - 1,)), dma((CROSS - 1,)),
         dma((CROSS - 1,)), dma((CROSS - 1,)),
-        dma((2, GROUP - 1)), dma((2, GROUP - 1)),
-        dma((3,)), dma((3,)),
+        dma((8,)), dma((8,)),
+        dma((2, 3)), dma((2, 3)),
         dma((2,)), dma((4,)),
     ]
     att, gw, gh = pl.pallas_call(
@@ -487,13 +554,21 @@
             jax.ShapeDtypeStruct((width, full), BF16),
             jax.ShapeDtypeStruct((width, rows), BF16),
         ),
-        in_specs=[pl.BlockSpec(memory_space=pl.ANY)] * 5,
+        in_specs=[pl.BlockSpec(memory_space=pltpu.HBM)] * 5,
         out_specs=[pl.BlockSpec(memory_space=pltpu.VMEM)] * 3,
         scratch_shapes=scratch,
         compiler_params=pltpu.CompilerParams(
-            collective_id=0, has_side_effects=True, vmem_limit_bytes=40 * 2**20
+            collective_id=0, has_side_effects=True, vmem_limit_bytes=60 * 2**20
         ),
     )(hidden_states.T, w_query.T, w_key.T, w_value.T, grad_out.T)
+    att, gw, gh = pl.pallas_call(
+        hand_out,
+        out_shape=tuple(jax.ShapeDtypeStruct(a.shape, BF16) for a in (att, gw, gh)),
+        in_specs=[pl.BlockSpec(memory_space=pltpu.HBM)] * 3,
+        out_specs=[pl.BlockSpec(memory_space=pltpu.HBM)] * 3,
+        scratch_shapes=[vm(a.shape, BF16) for a in (att, gw, gh)] + [dma((2, 3))],
+        compiler_params=pltpu.CompilerParams(vmem_limit_bytes=60 * 2**20),
+    )(att, gw, gh)
     return att.T, gw.T, gh.T
 
 

time: 72.6 us -> 63 us (0.87)
  the two profiles are of different devices: /device:TPU:1 before, /device:TPU:64 now
where the time goes in v2:
time: 63 us; the launch traced here: 62.8 us
  Pallas kernels  62.2 us (99%)
  between operations  0.64 us (1%)
    pallas_call x1, Pallas kernels, shards(): pl.pallas_call(kernel, out_shape=(jax.ShapeDtypeStruct((width, rows), BF1...  60 us
    pallas_call x1, Pallas kernels, shards(): pl.pallas_call(hand_out, out_shape=tuple((jax.ShapeDtypeStruct(a.shape, B...  2.15 us

profile of v2, /device:TPU:64, one launch (start us, length us, event | category | flops | bytes accessed | tf_op | source)
XLA Modules:
  0.0 62.8 jit_solution(9475713861331071605)
XLA Ops:
  0.6 60.0 %shard_map.76 = (bf16[320,128]{1,0:T(8,128)(2,1)}, bf16[320,1280]{1,0:T(8,128)(2,1)}, bf16[320,128]{1,0:T(8,128)(2,1)}) custom-call(bf16[320,128]{1,0:T(8,128)(2,1)} %bitcast.11, bf16[320,1280]{1,0:T(8,128)(2,1)} %bitcast.8, bf16[320,1280]{1,0:T(8,128)(2,1)} %bitcast.9, bf16[320,1280]{1,0:T(8,128)(2,1)} %bitcast.10, bf16[320,128]{1,0:T(8,128)(2,1)} %bitcast.12), custom_call_target="tpu_custom_call" | custom-call | tf_op jit(solution)/shard_map/pallas_call | solution.py:550
  60.6 2.2 %shard_map.77 = (bf16[320,128]{1,0:T(8,128)(2,1)}, bf16[320,1280]{1,0:T(8,128)(2,1)}, bf16[320,128]{1,0:T(8,128)(2,1)}) custom-call(bf16[320,128]{1,0:T(8,128)(2,1)} %get-tuple-element.9.refs_0_, bf16[320,1280]{1,0:T(8,128)(2,1)} %get-tuple-element.10.refs_1_, bf16[320,128]{1,0:T(8,128)(2,1)} %get-tuple-element.11.refs_2_), custom_call_target="tpu_custom_call" | custom-call | tf_op jit(solution)/shard_map/pallas_call | solution.py:564

commit v3 on v2

--- a/solution.py
+++ b/solution.py
@@ -161,7 +161,7 @@
 
     @pl.when(place == 0)
     def _():
-        for p in range(1, SPAN):
+        for p in reversed(range(1, SPAN)):
             lead_out(p).start()
 
     @pl.when(place < SPAN - 1)
@@ -286,16 +286,25 @@
 
     for r in range(1, GROUP):
         by_tiles(pos, lambda tiles, r=r: fe(r, pos, tiles).wait_recv())
-    for r in range(1, GROUP):
-        cc(r).wait_recv()
-    window = mm_nt(
-        jnp.concatenate([dqall[r] for r in range(GROUP)], 1),
-        jnp.concatenate([fall[r] for r in range(GROUP)], 1),
-    ).astype(BF16)
+    near_blocks, far_blocks = (0, 1, 7, 2), (6, 3, 5, 4)
+
+    def products(blocks):
+        for r in blocks:
+            if r:
+                cc(r).wait_recv()
+        return mm_nt(
+            jnp.concatenate([dqall[r] for r in blocks], 1),
+            jnp.concatenate([fall[r] for r in blocks], 1),
+        )
+
+    window = products(near_blocks)
+    window = (window + products(far_blocks)).astype(BF16)
     for k in range(15):
         i, l = k // 3, k % 3
         part[k] = window[32 * i : 32 * i + 32, 128 * l : 128 * l + 128]
-    part[15] = jnp.zeros((32, 128), BF16)
+
+    def holds(k):
+        return (k < 15) & (is_wide(pos) | (k % 3 < 2))
 
     def ee(r):
         return copy(
@@ -303,7 +312,7 @@
         )
 
     for r in CROSS_FAR_FIRST:
-        ee(r).start()
+        pl.when(holds(cross_pos(r)))(lambda r=r: ee(r).start())
 
     dk_n = jnp.transpose(jnp.concatenate(dks, 0))
     dv_n = jnp.transpose(jnp.concatenate(dvs, 0))
@@ -321,11 +330,6 @@
         yt[0, cols, :] = jnp.transpose(terms.astype(BF16))
     for r in range(1, HEADS_AX):
         hh(r, 0).start()
-    for r in range(1, CROSS):
-        ee(r).wait_recv()
-    total = part[cross].astype(F32)
-    for r in range(1, CROSS):
-        total = total + parts_in[r - 1].astype(F32)
 
     def piece(k):
         return gw_ref.at[
@@ -333,9 +337,6 @@
             pl.ds(pl.multiple_of(win_start(pos) + 128 * (k % 3), 128), 128),
         ]
 
-    def holds(k):
-        return (k < 15) & (is_wide(pos) | (k % 3 < 2))
-
     def ff(r):
         return copy(piece(cross), piece(cross), f_s.at[r - 1], f_r.at[r - 1], cross_peer(r))
 
@@ -345,6 +346,10 @@
 
     @pl.when(holds(cross))
     def _():
+        total = part[cross].astype(F32)
+        for r in reversed(CROSS_FAR_FIRST):
+            ee(r).wait_recv()
+            total = total + parts_in[r - 1].astype(F32)
         gw_ref[
             pl.ds(pl.multiple_of(win_rows(pos) + 32 * (cross // 3), 32), 32),
             pl.ds(pl.multiple_of(win_start(pos) + 128 * (cross % 3), 128), 128),
@@ -357,6 +362,7 @@
         terms = mm(dk_n[128:], wt[width : 2 * width, cols]) + mm(dv_n[128:], wt[2 * width :, cols])
         terms = terms + mm(dq_n, wt[0:width, cols])
         yt[1, cols, :] = jnp.transpose(terms.astype(BF16))
+
     for r in range(1, HEADS_AX):
         hh(r, 1).start()
     for r in range(1, HEADS_AX):
@@ -401,23 +407,33 @@
         ref = region(j, tiles, first, rows)
         return copy(ref, ref, g_s.at[slot], g_r.at[slot], peer_at(d))
 
-    near = ((0, 2), (1, -2), (2, 1), (3, -1))
-    onward = (
-        (4, -2, 1, 0, half_w), (5, 2, -1, 0, half_w),
-        (6, -2, 2, 0, half_w // 2), (7, 2, -2, half_w // 2, half_w // 2),
+    half_r = half_w // 2
+    near = (
+        (0, 2, 0, half_r), (1, -2, half_r, half_r), (2, 2, half_r, half_r), (3, -2, 0, half_r),
+        (4, 1, 0, half_w), (5, -1, 0, half_w),
     )
-    for slot, d in near:
-        by_tiles(pos, lambda tiles, slot=slot, d=d: hop(slot, pos, d, tiles).start())
-    for slot, d in near[:2]:
-        by_tiles(at(-d), lambda tiles, slot=slot, d=d: hop(slot, at(-d), d, tiles).wait_recv())
-        for out, of, dist, first, rows in onward:
-            if of == -d:
-                by_tiles(
-                    at(of),
-                    lambda tiles, out=out, of=of, dist=dist, first=first, rows=rows: hop(
-                        out, at(of), dist, tiles, first, rows
-                    ).start(),
-                )
+    onward = {
+        0: ((6, -2, 2, 0, half_r), (7, -2, 1, 0, half_r)),
+        1: ((8, 2, -2, half_r, half_r), (9, 2, -1, half_r, half_r)),
+        2: ((10, -2, 1, half_r, half_r),),
+        3: ((11, 2, -1, 0, half_r),),
+    }
+
+    def start(slot, j, *how):
+        by_tiles(j, lambda tiles: hop(slot, j, how[0], tiles, *how[1:]).start())
+
+    def arrived(slot, j, *how):
+        by_tiles(j, lambda tiles: hop(slot, j, how[0], tiles, *how[1:]).wait_recv())
+
+    def left(slot, j, *how):
+        by_tiles(j, lambda tiles: hop(slot, j, how[0], tiles, *how[1:]).wait_send())
+
+    for slot, *how in near:
+        start(slot, pos, *how)
+    for slot, d, *rows in near[:4]:
+        arrived(slot, at(-d), d, *rows)
+        for out, of, *how in onward[slot]:
+            start(out, at(of), *how)
 
     for r in range(1, HEADS_AX):
         hh(r, 1).wait_recv()
@@ -442,15 +458,11 @@
     local = jnp.where((place == 0) & low_lanes(own.shape), extra + roll_half(extra), 0.0)
     gh_ref[...] = (own + local + unpack(lead_sum, prev_in)).astype(BF16)
 
-    for slot, d in near[2:]:
-        by_tiles(at(-d), lambda tiles, slot=slot, d=d: hop(slot, at(-d), d, tiles).wait_recv())
-    for out, of, dist, first, rows in onward:
-        by_tiles(
-            at(of - dist),
-            lambda tiles, out=out, of=of, dist=dist, first=first, rows=rows: hop(
-                out, at(of - dist), dist, tiles, first, rows
-            ).wait_recv(),
-        )
+    for slot, d, *rows in near[4:]:
+        arrived(slot, at(-d), d, *rows)
+    for sends in onward.values():
+        for out, of, dist, *rows in sends:
+            arrived(out, at(of - dist), dist, *rows)
 
     for r in range(1, HEADS_AX):
         a1(r).wait_send()
@@ -475,17 +487,13 @@
     for r in range(1, GROUP):
         by_tiles(group_pos(r), lambda tiles, r=r: fe(r, group_pos(r), tiles).wait_send())
         cc(r).wait_send()
-    for slot, d in near:
-        by_tiles(pos, lambda tiles, slot=slot, d=d: hop(slot, pos, d, tiles).wait_send())
-    for out, of, dist, first, rows in onward:
-        by_tiles(
-            at(of),
-            lambda tiles, out=out, of=of, dist=dist, first=first, rows=rows: hop(
-                out, at(of), dist, tiles, first, rows
-            ).wait_send(),
-        )
+    for slot, *how in near:
+        left(slot, pos, *how)
+    for sends in onward.values():
+        for out, of, *how in sends:
+            left(out, at(of), *how)
     for r in range(1, CROSS):
-        ee(r).wait_send()
+        pl.when(holds(cross_pos(r)))(lambda r=r: ee(r).wait_send())
 
     @pl.when(holds(cross))
     def _():
@@ -543,7 +551,7 @@
         dma((GROUP - 1,)), dma((GROUP - 1,)),
         dma((CROSS - 1,)), dma((CROSS - 1,)),
         dma((CROSS - 1,)), dma((CROSS - 1,)),
-        dma((8,)), dma((8,)),
+        dma((12,)), dma((12,)),
         dma((2, 3)), dma((2, 3)),
         dma((2,)), dma((4,)),
     ]

time: 63 us -> 61.6 us (0.978)
  the two profiles are of different devices: /device:TPU:64 before, /device:TPU:2 now
where the time goes in v3:
time: 61.6 us; the launch traced here: 61.5 us
  Pallas kernels  60.8 us (99%)
  between operations  0.64 us (1%)
    pallas_call x1, Pallas kernels, shards(): pl.pallas_call(kernel, out_shape=(jax.ShapeDtypeStruct((width, rows), BF1...  58.7 us
    pallas_call x1, Pallas kernels, shards(): pl.pallas_call(hand_out, out_shape=tuple((jax.ShapeDtypeStruct(a.shape, B...  2.15 us

profile of v3, /device:TPU:2, one launch (start us, length us, event | category | flops | bytes accessed | tf_op | source)
XLA Modules:
  0.0 61.5 jit_solution(17129904320014030219)
XLA Ops:
  0.6 58.7 %shard_map.76 = (bf16[320,128]{1,0:T(8,128)(2,1)}, bf16[320,1280]{1,0:T(8,128)(2,1)}, bf16[320,128]{1,0:T(8,128)(2,1)}) custom-call(bf16[320,128]{1,0:T(8,128)(2,1)} %bitcast.11, bf16[320,1280]{1,0:T(8,128)(2,1)} %bitcast.8, bf16[320,1280]{1,0:T(8,128)(2,1)} %bitcast.9, bf16[320,1280]{1,0:T(8,128)(2,1)} %bitcast.10, bf16[320,128]{1,0:T(8,128)(2,1)} %bitcast.12), custom_call_target="tpu_custom_call" | custom-call | tf_op jit(solution)/shard_map/pallas_call | solution.py:558
  59.3 2.2 %shard_map.77 = (bf16[320,128]{1,0:T(8,128)(2,1)}, bf16[320,1280]{1,0:T(8,128)(2,1)}, bf16[320,128]{1,0:T(8,128)(2,1)}) custom-call(bf16[320,128]{1,0:T(8,128)(2,1)} %get-tuple-element.9.refs_0_, bf16[320,1280]{1,0:T(8,128)(2,1)} %get-tuple-element.10.refs_1_, bf16[320,128]{1,0:T(8,128)(2,1)} %get-tuple-element.11.refs_2_), custom_call_target="tpu_custom_call" | custom-call | tf_op jit(solution)/shard_map/pallas_call | solution.py:572

commit v4 on v3

--- a/solution.py
+++ b/solution.py
@@ -237,10 +237,6 @@
             c_s.at[r - 1], c_r.at[r - 1], group_peer(r),
         )
 
-    def send_half(part):
-        for r in FAR_FIRST:
-            pl.when(group_pos(r) % 2 == part)(lambda r=r: cc(r).start())
-
     for i in range(heads_here):
         a, b = HD * i, HD * (i + 1)
         q = qkv[a:b, :]
@@ -268,9 +264,8 @@
         spread(p_lead.astype(BF16), p_second.astype(BF16), 2 * i + 1)
         k_wide = jnp.concatenate([kve[a:b, :], qkv[width + a : width + b, :]], 1)
         dqt[a:b, :] = mm(k_wide, pts[2 * i]).astype(BF16)
-        if a < half_w <= b:
-            send_half(0)
-    send_half(1)
+    for r in FAR_FIRST:
+        cc(r).start()
     dqall[0] = dqt[pl.ds(win_rows(pos), half_w), :]
 
 
@@ -458,56 +453,60 @@
     local = jnp.where((place == 0) & low_lanes(own.shape), extra + roll_half(extra), 0.0)
     gh_ref[...] = (own + local + unpack(lead_sum, prev_in)).astype(BF16)
 
+    for r in range(1, HEADS_AX):
+        a1(r).wait_send()
+        a3(r).wait_send()
+        hh(r, 0).wait_send()
+        hh(r, 1).wait_send()
+
+    @pl.when(place == 0)
+    def _():
+        for p in range(1, SPAN):
+            lead_out(p).wait_send()
+
+    @pl.when(place < SPAN - 1)
+    def _():
+        prev_out().wait_send()
+
+    @pl.when(place > 0)
+    def _():
+        lead_back(1).wait_send()
+        prev_back().wait_send()
+
+    for r in range(1, GROUP):
+        by_tiles(group_pos(r), lambda tiles, r=r: fe(r, group_pos(r), tiles).wait_send())
+        cc(r).wait_send()
+    for slot, *how in near:
+        left(slot, pos, *how)
+    for r in range(1, CROSS):
+        pl.when(holds(cross_pos(r)))(lambda r=r: ee(r).wait_send())
+
+    @pl.when(holds(cross))
+    def _():
+        for r in range(1, CROSS):
+            ff(r).wait_send()
+
     for slot, d, *rows in near[4:]:
         arrived(slot, at(-d), d, *rows)
     for sends in onward.values():
         for out, of, dist, *rows in sends:
             arrived(out, at(of - dist), dist, *rows)
-
-    for r in range(1, HEADS_AX):
-        a1(r).wait_send()
-        a3(r).wait_send()
-        hh(r, 0).wait_send()
-        hh(r, 1).wait_send()
-
-    @pl.when(place == 0)
-    def _():
-        for p in range(1, SPAN):
-            lead_out(p).wait_send()
-
-    @pl.when(place < SPAN - 1)
-    def _():
-        prev_out().wait_send()
-
-    @pl.when(place > 0)
-    def _():
-        lead_back(1).wait_send()
-        prev_back().wait_send()
-
-    for r in range(1, GROUP):
-        by_tiles(group_pos(r), lambda tiles, r=r: fe(r, group_pos(r), tiles).wait_send())
-        cc(r).wait_send()
-    for slot, *how in near:
-        left(slot, pos, *how)
     for sends in onward.values():
         for out, of, *how in sends:
             left(out, at(of), *how)
-    for r in range(1, CROSS):
-        pl.when(holds(cross_pos(r)))(lambda r=r: ee(r).wait_send())
-
-    @pl.when(holds(cross))
-    def _():
-        for r in range(1, CROSS):
-            ff(r).wait_send()
 
 
 def hand_out(*refs):
-    count = 3
-    arrays, outs, held, sem = refs[:count], refs[count : 2 * count], refs[2 * count : -1], refs[-1]
-    arrivals = [
-        pltpu.make_async_copy(arrays[i], held[i], sem.at[0, i]) for i in range(count)
-    ]
-    copies = [pltpu.make_async_copy(held[i], outs[i], sem.at[1, i]) for i in range(count)]
+    arrays, outs, held, sem = refs[:3], refs[3:6], refs[6:9], refs[9]
+    arrivals, copies = [], []
+    for i, chunks in ((1, 4), (0, 1), (2, 1)):
+        rows = arrays[i].shape[0] // chunks
+        for c in range(chunks):
+            at, n = pl.ds(c * rows, rows), len(copies)
+            arrivals.append(
+                pltpu.make_async_copy(arrays[i].at[at], held[i].at[at], sem.at[0, n])
+            )
+            copies.append(pltpu.make_async_copy(held[i].at[at], outs[i].at[at], sem.at[1, n]))
     for arrival in arrivals:
         arrival.start()
     for arrival, out in zip(arrivals, copies):
@@ -574,7 +573,7 @@
         out_shape=tuple(jax.ShapeDtypeStruct(a.shape, BF16) for a in (att, gw, gh)),
         in_specs=[pl.BlockSpec(memory_space=pltpu.HBM)] * 3,
         out_specs=[pl.BlockSpec(memory_space=pltpu.HBM)] * 3,
-        scratch_shapes=[vm(a.shape, BF16) for a in (att, gw, gh)] + [dma((2, 3))],
+        scratch_shapes=[vm(a.shape, BF16) for a in (att, gw, gh)] + [dma((2, 6))],
         compiler_params=pltpu.CompilerParams(vmem_limit_bytes=60 * 2**20),
     )(att, gw, gh)
     return att.T, gw.T, gh.T

time: 61.6 us -> 61.2 us (level)
  no operation moved by 1% of the time
where the time goes in v4:
time: 61.2 us; the launch traced here: 61.1 us
  Pallas kernels  60.4 us (99%)
  between operations  0.64 us (1%)
    pallas_call x1, Pallas kernels, shards(): pl.pallas_call(kernel, out_shape=(jax.ShapeDtypeStruct((width, rows), BF1...  58.4 us
    pallas_call x1, Pallas kernels, shards(): pl.pallas_call(hand_out, out_shape=tuple((jax.ShapeDtypeStruct(a.shape, B...  2.07 us

profile of v4, /device:TPU:2, one launch (start us, length us, event | category | flops | bytes accessed | tf_op | source)
XLA Modules:
  0.0 61.1 jit_solution(4963296395879133168)
XLA Ops:
  0.6 58.4 %shard_map.76 = (bf16[320,128]{1,0:T(8,128)(2,1)}, bf16[320,1280]{1,0:T(8,128)(2,1)}, bf16[320,128]{1,0:T(8,128)(2,1)}) custom-call(bf16[320,128]{1,0:T(8,128)(2,1)} %bitcast.11, bf16[320,1280]{1,0:T(8,128)(2,1)} %bitcast.8, bf16[320,1280]{1,0:T(8,128)(2,1)} %bitcast.9, bf16[320,1280]{1,0:T(8,128)(2,1)} %bitcast.10, bf16[320,128]{1,0:T(8,128)(2,1)} %bitcast.12), custom_call_target="tpu_custom_call" | custom-call | tf_op jit(solution)/shard_map/pallas_call | solution.py:557
  59.0 2.1 %shard_map.77 = (bf16[320,128]{1,0:T(8,128)(2,1)}, bf16[320,1280]{1,0:T(8,128)(2,1)}, bf16[320,128]{1,0:T(8,128)(2,1)}) custom-call(bf16[320,128]{1,0:T(8,128)(2,1)} %get-tuple-element.9.refs_0_, bf16[320,1280]{1,0:T(8,128)(2,1)} %get-tuple-element.10.refs_1_, bf16[320,128]{1,0:T(8,128)(2,1)} %get-tuple-element.11.refs_2_), custom_call_target="tpu_custom_call" | custom-call | tf_op jit(solution)/shard_map/pallas_call | solution.py:571

commit v5 on v4

--- a/solution.py
+++ b/solution.py
@@ -198,7 +198,7 @@
             fe_s.at[r - 1], fe_r.at[r - 1], group_peer(r),
         )
 
-    for r in FAR_FIRST:
+    for r in reversed(FAR_FIRST):
         by_tiles(group_pos(r), lambda tiles, r=r: fe(r, group_pos(r), tiles).start())
 
     @pl.when(is_wide(pos))

time: 61.2 us -> 61.6 us (level)
  no operation moved by 1% of the time
where the time goes in v5:
time: 61.6 us; the launch traced here: 61.5 us
  Pallas kernels  60.8 us (99%)
  between operations  0.64 us (1%)
    pallas_call x1, Pallas kernels, shards(): pl.pallas_call(kernel, out_shape=(jax.ShapeDtypeStruct((width, rows), BF1...  58.8 us
    pallas_call x1, Pallas kernels, shards(): pl.pallas_call(hand_out, out_shape=tuple((jax.ShapeDtypeStruct(a.shape, B...  2.07 us

profile of v5, /device:TPU:2, one launch (start us, length us, event | category | flops | bytes accessed | tf_op | source)
XLA Modules:
  0.0 61.5 jit_solution(2400861546198596219)
XLA Ops:
  0.6 58.8 %shard_map.76 = (bf16[320,128]{1,0:T(8,128)(2,1)}, bf16[320,1280]{1,0:T(8,128)(2,1)}, bf16[320,128]{1,0:T(8,128)(2,1)}) custom-call(bf16[320,128]{1,0:T(8,128)(2,1)} %bitcast.11, bf16[320,1280]{1,0:T(8,128)(2,1)} %bitcast.8, bf16[320,1280]{1,0:T(8,128)(2,1)} %bitcast.9, bf16[320,1280]{1,0:T(8,128)(2,1)} %bitcast.10, bf16[320,128]{1,0:T(8,128)(2,1)} %bitcast.12), custom_call_target="tpu_custom_call" | custom-call | tf_op jit(solution)/shard_map/pallas_call | solution.py:557
  59.4 2.1 %shard_map.77 = (bf16[320,128]{1,0:T(8,128)(2,1)}, bf16[320,1280]{1,0:T(8,128)(2,1)}, bf16[320,128]{1,0:T(8,128)(2,1)}) custom-call(bf16[320,128]{1,0:T(8,128)(2,1)} %get-tuple-element.9.refs_0_, bf16[320,1280]{1,0:T(8,128)(2,1)} %get-tuple-element.10.refs_1_, bf16[320,128]{1,0:T(8,128)(2,1)} %get-tuple-element.11.refs_2_), custom_call_target="tpu_custom_call" | custom-call | tf_op jit(solution)/shard_map/pallas_call | solution.py:571
